TPU v7x, 256 devices: a whole 4x4x8 slice. The times are simulated.
256 devices in a mesh: bucket: 16 (over z, core), replica: 16 (over y, x).
Axes of the slice: x: 4, y: 4, z: 8, core: 2. Of those that a mesh axis runs over, the one named last changes fastest.
Arguments:
- rows: bfloat16 [262144, 768], P(('bucket', 'replica')), may hold values from -40 to 40, as said below
- cell_ids: int32 [262144, 1], P(('bucket', 'replica')), may hold values from 0 to 15; in each aligned block of 1024 rows (0 to 1023, 1024 to 2047, ...) at most 128 rows name the same one
- start_basis: float32 [16, 768, 768], P('bucket'), may hold values from -0.1 to 1.1, as said below
Outputs:
- rotated: bfloat16 [262144, 768], P(('bucket', 'replica'))
Inputs may be any that keep to these rules, and one draw needn't show every extreme that they name: `cell_ids`: in the rows of one device no cell is named by more than 128 rows, a bound that some block reaches; every cell is named by some row. `rows`: A residual row: a column offset plus rough noise with column and row scales. `start_basis`: the identity plus small dense entries.
All inputs are finite; a program needn't handle non-finite values.
Results may differ from a plain program's by a relative error of at most 0.0049.
Values may be sent and summed in bfloat16 or wider, within the bound.
A program may use at most 128 MiB of HBM per device.

v0:
```python
import jax
import jax.numpy as jnp
from jax import lax
from jax.sharding import PartitionSpec as P

CELLS = 16
ITERS_NS = 3
CAP = 128


def cell_solve(factor, image):
    return jax.scipy.linalg.solve_triangular(factor, image.T, lower=True).T


def local_gram(image):
    return jnp.einsum("cji,cjk->cik", image, image, precision=lax.Precision.HIGHEST)


def orthonormal(image, gram_matrix):
    factor = jax.vmap(jnp.linalg.cholesky)(gram_matrix)
    return jax.vmap(cell_solve)(factor, image)


def body(rows, cell_ids, start_basis):
    width = rows.shape[1]
    flat_ids = cell_ids[:, 0]
    onehot = (flat_ids[:, None] == jnp.arange(CELLS, dtype=jnp.int32)[None, :]).astype(jnp.int32)
    slot = jnp.sum(jnp.cumsum(onehot, axis=0) * onehot, axis=1) - 1
    send_counts = jnp.sum(onehot, axis=0).astype(jnp.bfloat16)[:, None]
    buffer = jnp.zeros((CELLS, CAP, width), jnp.bfloat16).at[flat_ids, slot].set(rows)
    received, recv_counts = (
        lax.all_to_all(buffer, "bucket", split_axis=0, concat_axis=1, tiled=True),
        lax.all_to_all(send_counts, "bucket", split_axis=0, concat_axis=1, tiled=True),
    )
    count_part = jnp.sum(recv_counts.astype(jnp.float32), axis=1)
    sum_part = jnp.sum(received, axis=1, dtype=jnp.float32)
    square_part = jnp.einsum("crd,cre->cde", received, received, preferred_element_type=jnp.float32)
    count_all, sum_all, square_all = lax.psum((count_part, sum_part, square_part), "replica")
    divisor = jnp.maximum(count_all, 1.0)
    mean = sum_all / divisor[:, None]
    covariance = square_all / divisor[:, None, None] - mean[:, :, None] * mean[:, None, :]
    current = start_basis
    for step in range(ITERS_NS):
        image = jnp.einsum("cij,cjk->cik", covariance, current, precision=lax.Precision.HIGHEST)
        current = orthonormal(image, local_gram(image))
    rotation = current.astype(jnp.bfloat16)
    shift = jnp.einsum(
        "cd,cde->ce", mean, rotation.astype(jnp.float32), precision=lax.Precision.HIGHEST
    )
    product = jnp.einsum("crd,cde->cre", received, rotation, preferred_element_type=jnp.float32)
    rotated_slots = (product - shift[:, None, :]).astype(jnp.bfloat16)
    returned = lax.all_to_all(rotated_slots, "bucket", split_axis=1, concat_axis=0, tiled=True)
    return returned[flat_ids, slot]


def solution(mesh):
    placed = (
        P(("bucket", "replica"), None),
        P(("bucket", "replica"), None),
        P("bucket", None, None),
    )
    return jax.shard_map(
        body, mesh=mesh, in_specs=placed, out_specs=P(("bucket", "replica"), None), check_vma=False
    )
```

profile of v0, /device:TPU:1, one launch (start us, length us, event | category | flops | bytes accessed | tf_op | source)
XLA Modules:
  0.0 1191.3 jit_solution(7130248097209281491)
XLA Ops:
  7.4 4.5 reduce-window.6
  15.3 7.9 scatter_custom_fusion
  23.2 83.5 %all_to_all.31 = bf16[16,128,768]{2,1,0:T(8,128)(2,1)S(1)} all-to-all(bf16[16,128,768]{2,1,0:T(8,128)(2,1)} %bitcast.878), channel_id=1, replica_groups=mesh['bucket'=16,'replica'=16] {'bucket'}, dimensions={0} | all-to-all | bytes 6291456 | tf_op jit(solution)/shard_map/all_to_all | solution.py:32
  108.4 4.1 convolution_bitcast_fusion
  116.6 6.5 all-to-all-done.1
  126.2 34.4 %all-reduce.1 = (f32[1,768]{1,0:T(1,128)S(1)}, f32[1]{0:T(128)}) all-reduce(f32[1,768]{1,0:T(1,128)S(1)} %reduce_sum.45, f32[1]{0:T(128)} %bitcast.11), channel_id=1, replica_groups=mesh['bucket'=16,'replica'=16] {'replica'}, use_global_device_ids=true, to_apply=%region_9.10 | all-reduce | flops 769 | bytes 6152 | tf_op jit(solution)/shard_map/psum | solution.py:38
  161.3 49.2 %all-reduce.4.cloned.1.call-done = f32[1,768,768]{2,1,0:T(8,128)} async-done(((f32[1,768,768]{2,1,0:T(8,128)}), f32[1,768,768]{2,1,0:T(8,128)}) %all-reduce.4.cloned.1.call-update) | async-done | bytes 2359312 | tf_op jit(solution)/shard_map/psum | solution.py:38
  210.5 7.8 fusion.8
  218.3 6.3 fusion.214
  230.4 11.7 custom-call.67
  242.3 9.8 custom-call.68
  254.9 11.7 custom-call.69
  266.7 10.0 custom-call.70
  278.6 11.7 custom-call.71
  291.0 9.8 custom-call.72
  302.7 12.1 %custom-call.73 = f32[1,128,128]{2,1,0:T(8,128)S(1)} custom-call(f32[1,128,128]{2,1,0:T(8,128)S(1)} %cholesky.930), custom_call_target="Cholesky" | custom-call | tf_op jit(solution)/shard_map/vmap(jit(cholesky))/cholesky | solution.py:20
  315.6 9.8 custom-call.74
  327.1 11.7 custom-call.75
  339.6 9.8 custom-call.76
  350.9 11.9 custom-call.77
  371.7 17.6 %while.6 = (s32[]{:T(128)}, f32[1,768,768]{2,1,0:T(8,128)}, s32[6,2]{0,1:T(2,128)S(1)}, f32[6,1,128,128]{3,2,1,0:T(8,128)S(1)}, s32[]{:T(128)}) while((s32[]{:T(128)}, f32[1,768,768]{2,1,0:T(8,128)}, s32[6,2]{0,1:T(2,128)S(1)}, f32[6,1,128,128]{3,2,1,0:T(8,128)S(1)}, s32[]{:T(128)}) %tuple.115), condition=%wide.while_cond, body=%wide.while_body.sunk | while | flops 2 | bytes 131181 | solution.py:12
  389.3 59.0 %custom-call.78 = f32[1,6,128,128]{2,3,1,0:T(8,128)S(1)} custom-call(f32[1,6,128,128]{3,2,1,0:T(8,128)S(1)} %bitcast.892), custom_call_target="InvertDiagBlocksLowerTriangular" | custom-call | tf_op jit(solution)/shard_map/vmap(jit(_solve_triangular))/triangular_solve | solution.py:12
  457.4 3.6 fusion.64
  461.6 4.9 fusion.90
  467.0 6.1 fusion.6
  473.2 6.5 fusion.215
  485.1 11.7 custom-call.79
  497.0 9.8 custom-call.80
  509.6 11.7 custom-call.81
  522.7 10.2 custom-call.82
  534.8 11.7 custom-call.83
  547.2 9.8 custom-call.84
  559.0 11.9 custom-call.85
  571.5 9.8 custom-call.86
  583.1 11.7 custom-call.87
  595.6 9.8 custom-call.88
  606.9 12.1 %custom-call.89 = f32[1,128,128]{2,1,0:T(8,128)S(1)} custom-call(f32[1,128,128]{2,1,0:T(8,128)S(1)} %fusion.139), custom_call_target="Cholesky" | custom-call | tf_op jit(solution)/shard_map/vmap(jit(cholesky))/cholesky | solution.py:20
  627.3 18.0 %while.7 = (s32[]{:T(128)}, f32[1,768,768]{2,1,0:T(8,128)}, s32[6,2]{0,1:T(2,128)S(1)}, f32[6,1,128,128]{3,2,1,0:T(8,128)S(1)}, s32[]{:T(128)}) while((s32[]{:T(128)}, f32[1,768,768]{2,1,0:T(8,128)}, s32[6,2]{0,1:T(2,128)S(1)}, f32[6,1,128,128]{3,2,1,0:T(8,128)S(1)}, s32[]{:T(128)}) %tuple.126), condition=%wide.while_cond.clone, body=%wide.while_body.clone.sunk | while | flops 2 | bytes 131181 | solution.py:12
  645.2 59.0 %custom-call.90 = f32[1,6,128,128]{2,3,1,0:T(8,128)S(1)} custom-call(f32[1,6,128,128]{3,2,1,0:T(8,128)S(1)} %bitcast.893), custom_call_target="InvertDiagBlocksLowerTriangular" | custom-call | tf_op jit(solution)/shard_map/vmap(jit(_solve_triangular))/triangular_solve | solution.py:12
  717.5 4.7 fusion.84
  722.7 6.1 fusion.4
  728.8 6.7 fusion.216
  740.9 11.7 custom-call.91
  752.8 9.8 custom-call.92
  765.4 11.7 custom-call.93
  778.5 9.9 custom-call.94
  790.4 11.7 custom-call.95
  802.8 9.8 custom-call.96
  814.5 12.1 %custom-call.97 = f32[1,128,128]{2,1,0:T(8,128)S(1)} custom-call(f32[1,128,128]{2,1,0:T(8,128)S(1)} %cholesky.976), custom_call_target="Cholesky" | custom-call | tf_op jit(solution)/shard_map/vmap(jit(cholesky))/cholesky | solution.py:20
  827.4 9.8 custom-call.98
  838.9 11.7 custom-call.99
  851.3 9.8 custom-call.100
  862.7 11.9 custom-call.101
  882.7 16.8 %while.8 = (s32[]{:T(128)}, f32[1,768,768]{2,1,0:T(8,128)}, s32[6,2]{0,1:T(2,128)S(1)}, f32[6,1,128,128]{3,2,1,0:T(8,128)S(1)}, s32[]{:T(128)}) while((s32[]{:T(128)}, f32[1,768,768]{2,1,0:T(8,128)}, s32[6,2]{0,1:T(2,128)S(1)}, f32[6,1,128,128]{3,2,1,0:T(8,128)S(1)}, s32[]{:T(128)}) %tuple.127), condition=%wide.while_cond.clone.1, body=%wide.while_body.clone.1.sunk | while | flops 2 | bytes 131181 | solution.py:12
  899.5 59.0 %custom-call.102 = f32[1,6,128,128]{2,3,1,0:T(8,128)S(1)} custom-call(f32[1,6,128,128]{3,2,1,0:T(8,128)S(1)} %bitcast.891), custom_call_target="InvertDiagBlocksLowerTriangular" | custom-call | tf_op jit(solution)/shard_map/vmap(jit(_solve_triangular))/triangular_solve | solution.py:12
  967.6 3.6 fusion.68
  971.7 4.7 fusion.78
  980.9 44.7 %copy.127 = bf16[1,2048,768]{2,0,1:T(2,128)(2,1)} copy(bf16[1,2048,768]{2,1,0:T(8,128)(2,1)S(1)} %fusion) | data formatting | bytes 6291456 | tf_op jit(solution)/shard_map/convert_element_type | solution.py:51
  1026.2 33.3 %reduce.53 = bf16[2048,768]{1,0:T(8,128)(2,1)} reduce(bf16[2048,1,768]{2,1,0:T(2,128)(2,1)} %bitcast.875, bf16[]{:T(256)} %broadcast.362), dimensions={1}, to_apply=%bitcast.833.reduce_sub_computation | reduce | bytes 6291458
  1059.4 6.4 reshape.753
  1065.8 82.1 %all_to_all.32 = bf16[16,2,49152]{2,1,0:T(2,128)(2,1)} all-to-all(bf16[16,2,49152]{2,1,0:T(2,128)(2,1)} %reshape.753), channel_id=1, replica_groups=mesh['bucket'=16,'replica'=16] {'bucket'}, dimensions={0} | all-to-all | bytes 6291456 | tf_op jit(solution)/shard_map/all_to_all | solution.py:52
  1147.9 11.5 reshape.754
  1159.4 5.0 copy.123
  1164.4 19.7 %gather_fusion = bf16[1024,768]{1,0:T(8,128)(2,1)} fusion(bf16[16,128,768]{2,1,0:T(8,128)(2,1)} %bitcast.852, s32[1024]{0:T(1024)S(1)} %bitcast.853), kind=kCustom, calls=%fused_computation | custom fusion | bytes 3153920 | tf_op jit(solution)/shard_map/gather | solution.py:53
  (240 shorter events, 173.2 us)
Async XLA Ops:
  6.5 204.0 %copy-start = (f32[1,768,768]{2,1,0:T(8,128)S(1)}, f32[1,768,768]{2,1,0:T(8,128)}, u32[]{:S(2)}) copy-start(f32[1,768,768]{2,1,0:T(8,128)} %param.8) | copy-start | bytes 7077892
  6.5 204.0 %all-reduce.4.cloned.1.call-start = ((), (), s32[]{:S(2)}) async-start(), calls=%async_computation.3 | async-start | bytes 4718592 | tf_op jit(solution)/shard_map/psum | solution.py:38
  106.7 1.7 copy-start.11
  113.2 9.8 all-to-all-start.1
  218.3 6.3 copy-start.4
  228.9 1.5 copy-start.15
  362.8 5.4 copy-start.8
  368.2 80.1 %copy-start.5 = (f32[768,768]{1,0:T(8,128)S(1)}, f32[768,768]{1,0:T(8,128)}, u32[]{:S(2)}) copy-start(f32[768,768]{1,0:T(8,128)} %copy-done.4) | copy-start | bytes 7077892
  461.0 6.0 copy-start.16
  473.1 6.5 copy-start.6
  483.6 1.5 copy-start.13
  619.1 4.7 copy-start.9
  623.8 80.4 %copy-start.7 = (f32[768,768]{1,0:T(8,128)S(1)}, f32[768,768]{1,0:T(8,128)}, u32[]{:S(2)}) copy-start(f32[768,768]{1,0:T(8,128)} %copy-done.6) | copy-start | bytes 7077892
  716.9 5.7 copy-start.17
  728.8 6.8 copy-start.2
  739.5 1.4 copy-start.14
  874.6 4.6 copy-start.10
  879.2 79.3 %copy-start.3 = (f32[768,768]{1,0:T(8,128)S(1)}, f32[768,768]{1,0:T(8,128)}, u32[]{:S(2)}) copy-start(f32[768,768]{1,0:T(8,128)} %copy-done.2) | copy-start | bytes 7077892
  971.7 6.3 copy-start.12
  1164.4 19.7 %copy-start.1 = (f32[1,768,768]{2,1,0:T(8,128)S(1)}, f32[1,768,768]{2,1,0:T(8,128)}, u32[]{:S(2)}) copy-start(f32[1,768,768]{2,1,0:T(8,128)} %param.8) | copy-start | bytes 7077892
Sparse Core Ops, SparseCore 0:
  112.6 97.8 all-reduce.3
where the time goes:
time: 1200 us; the launch traced here: 1190 us
  other arithmetic  611 us (51%)
  blocking collectives  200 us (17%)
  local copies, waits for them, and re-layouts  162 us (14%)
  matrix products  132 us (11%)
  waiting for transfers between devices  55.7 us (5%)
  between operations  27 us (2%)
    another operation x68, other arithmetic, orthonormal(): factor = jax.vmap(jnp.linalg.cholesky)(gram_matrix)  373 us
    another operation x7, other arithmetic, cell_solve(): return jax.scipy.linalg.solve_triangular(factor, image.T, lower=True).T  187 us
    all_to_all x1, blocking collectives, body(): lax.all_to_all(buffer, 'bucket', split_axis=0, concat_axis=1, tiled=True)  83.5 us
    all_to_all x1, blocking collectives, body(): lax.all_to_all(rotated_slots, 'bucket', split_axis=1, concat_axis=0, tile...  82.1 us
    another operation x33, matrix products, cell_solve(): return jax.scipy.linalg.solve_triangular(factor, image.T, lower=True).T  55.3 us
    another operation x58, local copies, waits for them, and re-layouts, cell_solve(): return jax.scipy.linalg.solve_triangular(factor, image.T, lower=True).T  52.1 us
    psum x1, waiting for transfers between devices, body(): lax.psum((count_part, sum_part, square_part), 'replica')  49.2 us
    convert_element_type x1, local copies, waits for them, and re-layouts, body(): rotated_slots = (product - shift[:, None, :]).astype(jnp.bfloat16)  44.7 us
  transfers between devices with their start and end apart: 2, of which 2 were waited for; matrix products, arithmetic and copies ran while one was open for 0% of the time, Pallas kernels for 0%

commit v1 on v0

--- a/solution.py
+++ b/solution.py
@@ -29,7 +29,12 @@
     send_counts = jnp.sum(onehot, axis=0).astype(jnp.bfloat16)[:, None]
     buffer = jnp.zeros((CELLS, CAP, width), jnp.bfloat16).at[flat_ids, slot].set(rows)
     received, recv_counts = (
-        lax.all_to_all(buffer, "bucket", split_axis=0, concat_axis=1, tiled=True),
+        jnp.concatenate(
+            lax.all_to_all(
+                jnp.stack(jnp.split(buffer, lax.axis_size("bucket"), axis=0)), "bucket", 0, 0
+            ),
+            axis=1,
+        ),
         lax.all_to_all(send_counts, "bucket", split_axis=0, concat_axis=1, tiled=True),
     )
     count_part = jnp.sum(recv_counts.astype(jnp.float32), axis=1)

time: 1200 us -> 1220 us (1.017)
  local copies, waits for them, and re-layouts: 162 us -> 177 us
    unnamed x41 -> x56, local copies, waits for them, and re-layouts: 37.3 us -> 51.4 us
where the time goes in v1:
time: 1220 us; the launch traced here: 1210 us
  other arithmetic  611 us (50%)
  blocking collectives  200 us (16%)
  local copies, waits for them, and re-layouts  177 us (15%)
  matrix products  132 us (11%)
  waiting for transfers between devices  55.6 us (5%)
  between operations  27.1 us (2%)
    another operation x68, other arithmetic, orthonormal(): factor = jax.vmap(jnp.linalg.cholesky)(gram_matrix)  373 us
    another operation x7, other arithmetic, cell_solve(): return jax.scipy.linalg.solve_triangular(factor, image.T, lower=True).T  187 us
    all_to_all x1, blocking collectives, body(): lax.all_to_all(jnp.stack(jnp.split(buffer, lax.axis_size('bucket'), axis=...  83.3 us
    all_to_all x1, blocking collectives, body(): lax.all_to_all(rotated_slots, 'bucket', split_axis=1, concat_axis=0, tile...  82.1 us
    another operation x33, matrix products, cell_solve(): return jax.scipy.linalg.solve_triangular(factor, image.T, lower=True).T  55.3 us
    another operation x58, local copies, waits for them, and re-layouts, cell_solve(): return jax.scipy.linalg.solve_triangular(factor, image.T, lower=True).T  52.1 us
    unnamed x56, local copies, waits for them, and re-layouts  51.4 us
    psum x1, waiting for transfers between devices, body(): lax.psum((count_part, sum_part, square_part), 'replica')  49.1 us
  transfers between devices with their start and end apart: 2, of which 2 were waited for; matrix products, arithmetic and copies ran while one was open for 0% of the time, Pallas kernels for 0%

profile of v1, /device:TPU:1, one launch (start us, length us, event | category | flops | bytes accessed | tf_op | source)
XLA Modules:
  0.0 1206.1 jit_solution(6375242782734492808)
XLA Ops:
  7.4 4.5 reduce-window.6
  15.3 7.9 scatter_custom_fusion
  38.4 83.3 %all_to_all.27 = bf16[16,1,128,768]{3,2,1,0:T(8,128)(2,1)S(1)} all-to-all(bf16[16,1,128,768]{3,2,1,0:T(8,128)(2,1)S(1)} %fusion.163), channel_id=1, replica_groups=mesh['bucket'=16,'replica'=16] {'bucket'}, dimensions={0} | all-to-all | bytes 6291456 | tf_op jit(solution)/shard_map/all_to_all | solution.py:33
  123.3 4.1 fusion.21
  131.5 6.5 all-to-all-done.1
  141.1 34.5 %all-reduce.1 = (f32[1,768]{1,0:T(1,128)S(1)}, f32[1]{0:T(128)}) all-reduce(f32[1,768]{1,0:T(1,128)S(1)} %reduce_sum.45, f32[1]{0:T(128)} %bitcast.27), channel_id=1, replica_groups=mesh['bucket'=16,'replica'=16] {'replica'}, use_global_device_ids=true, to_apply=%region_9.10 | all-reduce | flops 769 | bytes 6152 | tf_op jit(solution)/shard_map/psum | solution.py:43
  176.3 49.1 %all-reduce.4.cloned.1.call-done = f32[1,768,768]{2,1,0:T(8,128)} async-done(((f32[1,768,768]{2,1,0:T(8,128)}), f32[1,768,768]{2,1,0:T(8,128)}) %all-reduce.4.cloned.1.call-update) | async-done | bytes 2359312 | tf_op jit(solution)/shard_map/psum | solution.py:43
  225.4 7.8 fusion.10
  233.2 6.3 fusion.235
  245.3 11.7 custom-call.67
  257.2 9.8 custom-call.68
  269.8 11.7 custom-call.69
  281.6 10.0 custom-call.70
  293.4 11.7 custom-call.71
  305.9 9.8 custom-call.72
  317.6 12.1 %custom-call.73 = f32[1,128,128]{2,1,0:T(8,128)S(1)} custom-call(f32[1,128,128]{2,1,0:T(8,128)S(1)} %cholesky.930), custom_call_target="Cholesky" | custom-call | tf_op jit(solution)/shard_map/vmap(jit(cholesky))/cholesky | solution.py:20
  330.4 9.8 custom-call.74
  342.0 11.7 custom-call.75
  354.4 9.8 custom-call.76
  365.8 11.9 custom-call.77
  386.6 17.6 %while.6 = (s32[]{:T(128)}, f32[1,768,768]{2,1,0:T(8,128)}, s32[6,2]{0,1:T(2,128)S(1)}, f32[6,1,128,128]{3,2,1,0:T(8,128)S(1)}, s32[]{:T(128)}) while((s32[]{:T(128)}, f32[1,768,768]{2,1,0:T(8,128)}, s32[6,2]{0,1:T(2,128)S(1)}, f32[6,1,128,128]{3,2,1,0:T(8,128)S(1)}, s32[]{:T(128)}) %tuple.115), condition=%wide.while_cond, body=%wide.while_body.sunk | while | flops 2 | bytes 131181 | solution.py:12
  404.2 59.0 %custom-call.78 = f32[1,6,128,128]{2,3,1,0:T(8,128)S(1)} custom-call(f32[1,6,128,128]{3,2,1,0:T(8,128)S(1)} %bitcast.957), custom_call_target="InvertDiagBlocksLowerTriangular" | custom-call | tf_op jit(solution)/shard_map/vmap(jit(_solve_triangular))/triangular_solve | solution.py:12
  472.3 3.6 fusion.69
  476.4 4.9 fusion.95
  481.9 6.1 fusion.8
  488.0 6.5 fusion.236
  500.0 11.7 custom-call.79
  511.9 9.8 custom-call.80
  524.5 11.7 custom-call.81
  537.6 10.2 custom-call.82
  549.7 11.7 custom-call.83
  562.1 9.8 custom-call.84
  573.8 11.9 custom-call.85
  586.4 9.8 custom-call.86
  598.0 11.7 custom-call.87
  610.5 9.8 custom-call.88
  621.8 12.1 %custom-call.89 = f32[1,128,128]{2,1,0:T(8,128)S(1)} custom-call(f32[1,128,128]{2,1,0:T(8,128)S(1)} %fusion.144), custom_call_target="Cholesky" | custom-call | tf_op jit(solution)/shard_map/vmap(jit(cholesky))/cholesky | solution.py:20
  642.2 18.0 %while.7 = (s32[]{:T(128)}, f32[1,768,768]{2,1,0:T(8,128)}, s32[6,2]{0,1:T(2,128)S(1)}, f32[6,1,128,128]{3,2,1,0:T(8,128)S(1)}, s32[]{:T(128)}) while((s32[]{:T(128)}, f32[1,768,768]{2,1,0:T(8,128)}, s32[6,2]{0,1:T(2,128)S(1)}, f32[6,1,128,128]{3,2,1,0:T(8,128)S(1)}, s32[]{:T(128)}) %tuple.126), condition=%wide.while_cond.clone, body=%wide.while_body.clone.sunk | while | flops 2 | bytes 131181 | solution.py:12
  660.1 59.0 %custom-call.90 = f32[1,6,128,128]{2,3,1,0:T(8,128)S(1)} custom-call(f32[1,6,128,128]{3,2,1,0:T(8,128)S(1)} %bitcast.958), custom_call_target="InvertDiagBlocksLowerTriangular" | custom-call | tf_op jit(solution)/shard_map/vmap(jit(_solve_triangular))/triangular_solve | solution.py:12
  732.4 4.7 fusion.89
  737.6 6.1 fusion.6
  743.7 6.7 fusion.237
  755.7 11.7 custom-call.91
  767.7 9.8 custom-call.92
  780.3 11.7 custom-call.93
  793.4 9.9 custom-call.94
  805.3 11.7 custom-call.95
  817.7 9.8 custom-call.96
  829.4 12.1 %custom-call.97 = f32[1,128,128]{2,1,0:T(8,128)S(1)} custom-call(f32[1,128,128]{2,1,0:T(8,128)S(1)} %cholesky.976), custom_call_target="Cholesky" | custom-call | tf_op jit(solution)/shard_map/vmap(jit(cholesky))/cholesky | solution.py:20
  842.2 9.8 custom-call.98
  853.8 11.7 custom-call.99
  866.2 9.8 custom-call.100
  877.6 11.9 custom-call.101
  897.6 16.8 %while.8 = (s32[]{:T(128)}, f32[1,768,768]{2,1,0:T(8,128)}, s32[6,2]{0,1:T(2,128)S(1)}, f32[6,1,128,128]{3,2,1,0:T(8,128)S(1)}, s32[]{:T(128)}) while((s32[]{:T(128)}, f32[1,768,768]{2,1,0:T(8,128)}, s32[6,2]{0,1:T(2,128)S(1)}, f32[6,1,128,128]{3,2,1,0:T(8,128)S(1)}, s32[]{:T(128)}) %tuple.127), condition=%wide.while_cond.clone.1, body=%wide.while_body.clone.1.sunk | while | flops 2 | bytes 131181 | solution.py:12
  914.4 59.0 %custom-call.102 = f32[1,6,128,128]{2,3,1,0:T(8,128)S(1)} custom-call(f32[1,6,128,128]{3,2,1,0:T(8,128)S(1)} %bitcast.956), custom_call_target="InvertDiagBlocksLowerTriangular" | custom-call | tf_op jit(solution)/shard_map/vmap(jit(_solve_triangular))/triangular_solve | solution.py:12
  982.5 3.6 fusion.73
  986.6 4.7 fusion.83
  995.8 44.7 %copy.142 = bf16[1,2048,768]{2,0,1:T(2,128)(2,1)} copy(bf16[1,2048,768]{2,1,0:T(8,128)(2,1)S(1)} %fusion.2) | data formatting | bytes 6291456 | tf_op jit(solution)/shard_map/convert_element_type | solution.py:56
  1041.1 33.3 %reduce.53 = bf16[2048,768]{1,0:T(8,128)(2,1)} reduce(bf16[2048,1,768]{2,1,0:T(2,128)(2,1)} %bitcast.941, bf16[]{:T(256)} %broadcast.362), dimensions={1}, to_apply=%bitcast.899.reduce_sub_computation | reduce | bytes 6291458
  1074.3 6.4 reshape.788
  1080.7 82.1 %all_to_all.28 = bf16[16,2,49152]{2,1,0:T(2,128)(2,1)} all-to-all(bf16[16,2,49152]{2,1,0:T(2,128)(2,1)} %reshape.788), channel_id=1, replica_groups=mesh['bucket'=16,'replica'=16] {'bucket'}, dimensions={0} | all-to-all | bytes 6291456 | tf_op jit(solution)/shard_map/all_to_all | solution.py:57
  1162.8 11.5 reshape.789
  1174.2 5.0 copy.138
  1179.2 19.7 %gather_fusion = bf16[1024,768]{1,0:T(8,128)(2,1)} fusion(bf16[16,128,768]{2,1,0:T(8,128)(2,1)} %bitcast.918, s32[1024]{0:T(1024)S(1)} %bitcast.919), kind=kCustom, calls=%fused_computation | custom fusion | bytes 3153920 | tf_op jit(solution)/shard_map/gather | solution.py:58
  (256 shorter events, 188.3 us)
Async XLA Ops:
  6.5 218.8 %copy-start = (f32[1,768,768]{2,1,0:T(8,128)S(1)}, f32[1,768,768]{2,1,0:T(8,128)}, u32[]{:S(2)}) copy-start(f32[1,768,768]{2,1,0:T(8,128)} %param.8) | copy-start | bytes 7077892
  6.5 218.8 %all-reduce.4.cloned.1.call-start = ((), (), s32[]{:S(2)}) async-start(), calls=%async_computation.3 | async-start | bytes 4718592 | tf_op jit(solution)/shard_map/psum | solution.py:43
  121.6 1.7 copy-start.11
  128.2 9.8 all-to-all-start.1
  233.1 6.3 copy-start.4
  243.8 1.5 copy-start.15
  377.7 5.4 copy-start.8
  383.1 80.1 %copy-start.5 = (f32[768,768]{1,0:T(8,128)S(1)}, f32[768,768]{1,0:T(8,128)}, u32[]{:S(2)}) copy-start(f32[768,768]{1,0:T(8,128)} %copy-done.4) | copy-start | bytes 7077892
  475.9 6.0 copy-start.16
  488.0 6.5 copy-start.6
  498.5 1.5 copy-start.13
  633.9 4.7 copy-start.9
  638.6 80.4 %copy-start.7 = (f32[768,768]{1,0:T(8,128)S(1)}, f32[768,768]{1,0:T(8,128)}, u32[]{:S(2)}) copy-start(f32[768,768]{1,0:T(8,128)} %copy-done.6) | copy-start | bytes 7077892
  731.8 5.7 copy-start.17
  743.7 6.8 copy-start.2
  754.3 1.4 copy-start.14
  889.5 4.6 copy-start.10
  894.1 79.3 %copy-start.3 = (f32[768,768]{1,0:T(8,128)S(1)}, f32[768,768]{1,0:T(8,128)}, u32[]{:S(2)}) copy-start(f32[768,768]{1,0:T(8,128)} %copy-done.2) | copy-start | bytes 7077892
  986.6 6.3 copy-start.12
  1179.2 19.7 %copy-start.1 = (f32[1,768,768]{2,1,0:T(8,128)S(1)}, f32[1,768,768]{2,1,0:T(8,128)}, u32[]{:S(2)}) copy-start(f32[1,768,768]{2,1,0:T(8,128)} %param.8) | copy-start | bytes 7077892
Sparse Core Ops, SparseCore 0:
  127.6 97.7 all-reduce.3
